TPU v7x, 256 devices: a whole 4x4x8 slice. The times are simulated.
256 devices in a mesh: clip: 2 (over x_hi), frame: 4 (over y), row: 32 (over x_lo, z, core).
Axes of the slice: x: 4 (x_hi: 2, x_lo: 2; x = x_hi * 2 + x_lo), y: 4, z: 8, core: 2. Of those that a mesh axis runs over, the one named last changes fastest.
Arguments:
- x_input: bfloat16 [2, 4, 256, 120, 128], P('clip', 'frame', 'row'), may hold values from -12 to 12
- d_output: bfloat16 [2, 4, 256, 120, 128], P('clip', 'frame', 'row'), may hold values from -8 to 8
- gain_one: float32 [120], replicated, may hold values from 0.1 to 1.9
- w_self: bfloat16 [120, 360], replicated, may hold values from -0.5 to 0.5
- w_mutual: bfloat16 [120, 360], replicated, may hold values from -0.5 to 0.5
- w_proj: bfloat16 [240, 120], replicated, may hold values from -0.375 to 0.375
- gain_two: float32 [120], replicated, may hold values from 0.1 to 1.9
- w_fc_one: bfloat16 [120, 240], replicated, may hold values from -0.5 to 0.5
- w_fc_two: bfloat16 [120, 240], replicated, may hold values from -0.5 to 0.5
- w_down: bfloat16 [240, 120], replicated, may hold values from -0.375 to 0.375
Outputs:
- grad_input: bfloat16 [2, 4, 256, 120, 128], P('clip', 'frame', 'row')
- grad_gain_one: float32 [120], replicated
- grad_w_self: float32 [120, 360], replicated
- grad_w_mutual: float32 [120, 360], replicated
- grad_w_proj: float32 [240, 120], replicated
- grad_gain_two: float32 [120], replicated
- grad_fc_one: float32 [120, 240], replicated
- grad_fc_two: float32 [120, 240], replicated
- grad_w_down: float32 [240, 120], replicated
All inputs are finite; a program needn't handle non-finite values.
Results may differ from a plain program's by a relative error of at most 0.013.
Values may be sent and summed in bfloat16 or wider, within the bound.
A program may use at most 128 MiB of HBM per device.

v0:
```python
import math

import jax
import jax.numpy as jnp
from jax import lax
from jax.experimental import pallas as pl
from jax.experimental.pallas import tpu as pltpu
from jax.sharding import PartitionSpec as P

F32 = jnp.float32
BF16 = jnp.bfloat16
MESH = pl.DeviceIdType.MESH

C = 120
L = 128
W = 128
HEADS = 6
HD = 20
MLP = 240
M = 256
T = 1024
HALF = 512
CH = 256
EPS = 1e-05
EXP_SCALE = float(HD) ** -0.5 * math.log2(math.e)
SCALE = float(HD) ** -0.5

EARLY = 8 * L
CROSS = EARLY
SELF = CROSS + 4 * L
ROWS = SELF + 4 * L


def nn(a, b):
    return lax.dot_general(a, b, (((1,), (0,)), ((), ())), preferred_element_type=F32)


def nt(a, b):
    return lax.dot_general(a, b, (((1,), (1,)), ((), ())), preferred_element_type=F32)


def iota(shape, dim):
    return lax.broadcasted_iota(jnp.int32, shape, dim)


def one_hot(mask):
    return jnp.where(mask, 1.0, 0.0).astype(BF16)


def pad_rows(v):
    return jnp.concatenate([v, jnp.zeros((L - C, v.shape[1]), F32)], axis=0).astype(BF16)


def norm_parts(v):
    mean = jnp.sum(v, axis=0, keepdims=True) * (1.0 / C)
    centre = v - mean
    var = jnp.sum(centre * centre, axis=0, keepdims=True) * (1.0 / C)
    inv = lax.rsqrt(var + EPS)
    return centre * inv, inv


def norm_back(xhat, inv, gain, dy):
    dh = dy * gain
    m1 = jnp.sum(dh, axis=0, keepdims=True) * (1.0 / C)
    m2 = jnp.sum(dh * xhat, axis=0, keepdims=True) * (1.0 / C)
    return inv * (dh - m1 - xhat * m2)


def gain_row(acc):
    full = jnp.concatenate([acc, jnp.zeros((L - C, L), F32)], axis=0)
    row = jnp.sum(jnp.transpose(full), axis=0, keepdims=True)
    return jnp.broadcast_to(row, (8, L))


def fold_lanes(v):
    out = v[:, :L]
    for i in range(1, v.shape[1] // L):
        out = out + v[:, i * L : (i + 1) * L]
    return out


def make_perms(split, join):
    o, i = iota((HALF, HALF), 1), iota((HALF, HALF), 0)
    column = (o >> 8) * 64 + ((o >> 5) & 7) * 8 + (o & 7) + 4
    split[...] = one_hot(i == ((o >> 3) & 3) * W + (column & (W - 1)))
    join[...] = one_hot(i == ((o >> 5) & 3) * L + (o >> 7) * 32 + (o & 31))


def make_masks(mask_h, mask_f):
    row, lane = iota((L, HEADS * L), 0), iota((L, HEADS * L), 1)
    h = lane >> 7
    mask_h[...] = one_hot((row >= h * HD) & (row < h * HD + HD))
    mask_f[...] = one_hot((row >> 6) != ((lane >> 6) & 1))


def make_weights(ws, wm, wp, f1, f2, wd, wn, wt, proj, proj_t, fc_n, fc_t, down):
    def rows128(ref):
        return pad_rows(ref[...].astype(F32))

    r, e = iota((3 * L, 3 * C), 0), iota((3 * L, 3 * C), 1)
    pad3 = one_hot((e == (r >> 7) * C + (r & (L - 1))) & ((r & (L - 1)) < C))
    for i, ref in enumerate((ws, wm)):
        w = rows128(ref)
        wt[pl.ds(i * 3 * L, 3 * L), :] = nt(pad3, w).astype(BF16)
        wn[:, pl.ds(i * 3 * L, 3 * L)] = nt(w, pad3).astype(BF16)
    r, e = iota((M, MLP), 0), iota((M, MLP), 1)
    pad_m = one_hot(r == e)
    pad2 = one_hot((e == (r >> 7) * C + (r & (L - 1))) & ((r & (L - 1)) < C))
    pad_l = one_hot(iota((C, L), 0) == iota((C, L), 1))
    eye = one_hot(iota((L, L), 0) == iota((L, L), 1))
    for i, ref in enumerate((f1, f2)):
        w = rows128(ref)
        fc_t[pl.ds(i * M, M), :] = nt(pad_m, w).astype(BF16)
        fc_n[:, pl.ds(i * M, M)] = nt(w, pad_m).astype(BF16)
    down[...] = nn(nn(pad_m, wd[...]).astype(BF16), pad_l).astype(BF16)
    padded = nn(nn(pad2, wp[...]).astype(BF16), pad_l).astype(BF16)
    proj[...] = padded
    proj_t[...] = nt(eye, padded).astype(BF16)


def make_gain(gain, col):
    col[...] = jnp.transpose(jnp.broadcast_to(gain[...], (L, C)))


def wide(col):
    return jnp.concatenate([col[...]] * (CH // L), axis=1)


def to_slab(slab, rows_ref):
    for i in range(8):
        slab[pl.ds((1 - i // 4) * L, C), pl.ds((i % 4) * W, W)] = rows_ref[i]


def split_blocks(slab, split, out):
    blocks = nn(slab[...], split[...]).astype(BF16)
    for part in range(2):
        for half in range(2):
            for u in range(2):
                first = half * CH + u * L
                out[u, 2 * part + half] = blocks[part * L : part * L + L, first : first + L]


def join_blocks(u, blocks, join, out):
    beside = jnp.concatenate([blocks[u, s] for s in range(4)], axis=1)
    out[:, pl.ds(u * HALF, HALF)] = nn(beside, join[...]).astype(BF16)


def norm_one(u, win, gain_col, out_cm, out_tm):
    gain = wide(gain_col)

    def step(i, carry):
        at = pl.ds(pl.multiple_of(i * CH, CH), CH)
        y = norm_parts(win[:, at].astype(F32)[:C])[0] * gain
        y = jnp.concatenate([y, jnp.zeros((L - C, CH), F32)], axis=0)
        out_cm[:, at] = y.astype(BF16)
        out_tm[at, :] = jnp.transpose(y).astype(BF16)
        return carry

    lax.fori_loop(u * 2, u * 2 + 2, step, 0, unroll=2)


def project(u, wt, wn, n_cm, n_tm, cm, tm):
    at = pl.ds(u * HALF, HALF)
    cm[:, at] = nn(wt[...], n_cm[:, at]).astype(BF16)
    tm[at, pl.ds(0, 2 * L)] = nn(n_tm[at, :], wn[:, pl.ds(L, 2 * L)]).astype(BF16)
    tm[at, pl.ds(2 * L, 2 * L)] = nn(n_tm[at, :], wn[:, pl.ds(4 * L, 2 * L)]).astype(BF16)


def spread(v, mask_h):
    return jnp.concatenate([v] * HEADS, axis=1) * mask_h[...]


def stacked(v):
    return jnp.concatenate([v[:, h * L : (h + 1) * L] for h in range(HEADS)], axis=0)


def other_frame(v):
    first = (iota((64, HEADS * L), 1) & 64) == 0
    return jnp.where(first, v[64:], v[:64])


def both_frames(v, mask_f):
    return jnp.concatenate([v, v], axis=0) * mask_f[...]


def softmax(scores):
    raised = jnp.exp2(scores * EXP_SCALE)
    return (raised * (1.0 / jnp.sum(raised, axis=0, keepdims=True))).astype(BF16)


def attend(cm, tm, mask_h, mask_f, probs, joined):
    def step(p, carry):
        at = pl.ds(pl.multiple_of(p * L, L), L)

        def group(i):
            return spread(cm[pl.ds(i * L, L), at], mask_h)

        pr = softmax(nn(tm[at, pl.ds(0, L)], group(0)))
        probs[p, pl.ds(0, L), :] = pr
        joined[pl.ds(L, L), at] = nn(group(2), stacked(pr)).astype(BF16)
        pr = softmax(other_frame(nn(tm[at, pl.ds(2 * L, L)], group(3))))
        pr = both_frames(pr, mask_f)
        probs[p, pl.ds(L, L), :] = pr
        joined[pl.ds(0, L), at] = nn(group(5), stacked(pr)).astype(BF16)
        return carry

    lax.fori_loop(0, T // L, step, 0, unroll=8)


def score_back(pr, d_pr):
    pr = pr.astype(F32)
    delta = jnp.sum(pr * d_pr, axis=0, keepdims=True)
    return (pr * (d_pr - delta)).astype(BF16)


def back_self(cm, tm, mask_h, probs, dj, dq, d_tm, between):
    def step(p, carry):
        at = pl.ds(pl.multiple_of(p * L, L), L)

        def group(i):
            return spread(cm[pl.ds(i * L, L), at], mask_h)

        pr = probs[p, pl.ds(0, L), :]
        do = spread(dj[pl.ds(L, L), at], mask_h)
        ds = score_back(pr, nn(tm[at, pl.ds(L, L)], do))
        dq[pl.ds(0, L), at] = (nn(group(1), stacked(ds)) * SCALE).astype(BF16)
        d_tm[at, pl.ds(0, L)] = (nt(ds, group(0)) * SCALE).astype(BF16)
        d_tm[at, pl.ds(L, L)] = nt(pr, do).astype(BF16)
        between(p)
        return carry

    lax.fori_loop(0, T // L, step, 0, unroll=8)


def back_cross(cm, tm, mask_h, probs, dj, dq, d_tm, mask_f, between):
    def step(p, carry):
        at = pl.ds(pl.multiple_of(p * L, L), L)

        def group(i):
            return spread(cm[pl.ds(i * L, L), at], mask_h)

        pr = probs[p, pl.ds(L, L), :]
        do = spread(dj[pl.ds(0, L), at], mask_h)
        ds = score_back(pr[:64] + pr[64:], other_frame(nn(tm[at, pl.ds(3 * L, L)], do)))
        ds = both_frames(ds, mask_f)
        dq[pl.ds(L, L), at] = (nn(group(4), stacked(ds)) * SCALE).astype(BF16)
        d_tm[at, pl.ds(2 * L, L)] = (nt(ds, group(3)) * SCALE).astype(BF16)
        d_tm[at, pl.ds(3 * L, L)] = nt(pr, do).astype(BF16)
        between(p)
        return carry

    lax.fori_loop(0, T // L, step, 0, unroll=8)


def feed_forward(
    win, d_win, joined, gain_col, proj, proj_t, fc_n, fc_t, down, hid, dup, n2, datt, dres, dj, acc
):
    gain = wide(gain_col)
    acc[...] = jnp.zeros_like(acc)

    def step(i, carry):
        at = pl.ds(pl.multiple_of(i * CH, CH), CH)
        att = nn(proj_t[...], joined[:, at]).astype(BF16).astype(F32)
        xhat, inv = norm_parts(win[:, at].astype(F32)[:C] + att[:C])
        normed = pad_rows(xhat * gain)
        n2[:, at] = normed
        up = nn(fc_t[...], normed)
        up_one, up_two = up[:M], up[M:]
        cdf = 0.5 * (1.0 + lax.erf(up_one * math.sqrt(0.5)))
        gelu = up_one * cdf
        slope = cdf + up_one * (
            jnp.exp2(up_one * up_one * (-0.5 * math.log2(math.e))) * (1.0 / math.sqrt(2.0 * math.pi))
        )
        hid[:, at] = (gelu * up_two).astype(BF16)
        grad = d_win[:, at]
        d_hid = nn(down[...], grad).astype(BF16).astype(F32)
        d_up = jnp.concatenate(
            [(d_hid * up_two * slope).astype(BF16), (d_hid * gelu).astype(BF16)], axis=0
        )
        dup[:, at] = d_up
        dn = nn(fc_n[...], d_up).astype(BF16).astype(F32)[:C]
        acc[...] += fold_lanes(dn * xhat)
        d_resid = grad.astype(F32)[:C] + norm_back(xhat, inv, gain, dn)
        dres[:, at] = d_resid
        da = pad_rows(d_resid)
        datt[:, at] = da
        dj[:, at] = nn(proj[...], da).astype(BF16)
        return carry

    lax.fori_loop(0, T // CH, step, 0, unroll=4)


def early_grads(hid, dup, n2, joined, datt, d_win, acc, pack):
    g = nt(hid[...], d_win[...])
    row = gain_row(acc[...])
    g = jnp.concatenate([g[:MLP], row, row], axis=0)
    pack[pl.ds(0, 2 * L), :] = g.astype(BF16)
    for i in range(2):
        g = nt(n2[...], dup[pl.ds(i * M, M), :]).astype(BF16)
        pack[pl.ds((2 + 2 * i) * L, L), :] = g[:, :L]
        pack[pl.ds((3 + 2 * i) * L, L), :] = g[:, L:]
    pack[pl.ds(6 * L, 2 * L), :] = nt(joined[...], datt[...]).astype(BF16)


def put_grads(pack, base, grads):
    for i, g in enumerate(grads):
        pack[pl.ds(base + i * L, L), :] = g.astype(BF16)
    pack[pl.ds(base + 3 * L, L), :] = jnp.zeros((L, L), BF16)


def by_weights(grads, wn, first):
    acc = jnp.zeros((L, L), F32)
    for i, g in enumerate(grads):
        acc = acc + g * wn[:, pl.ds((first + i) * L, L)].astype(F32)
    return acc[:C]


def cross_grads(n_cm, dq, d_tm, wn, pack, acc):
    g = nn(n_cm[...], d_tm[:, pl.ds(2 * L, 2 * L)])
    grads = [nt(n_cm[...], dq[pl.ds(L, L), :]), g[:, :L], g[:, L:]]
    put_grads(pack, CROSS, grads)
    acc[...] = by_weights(grads, wn, 3)


def self_grads(n_cm, dq, d_tm, wn, pack, acc, col):
    g = nn(n_cm[...], d_tm[:, pl.ds(0, 2 * L)])
    grads = [nt(n_cm[...], dq[pl.ds(0, L), :]), g[:, :L], g[:, L:]]
    row = gain_row((by_weights(grads, wn, 0) + acc[...]) / col[...])
    grads[0] = jnp.concatenate([grads[0][:C], row], axis=0)
    put_grads(pack, SELF, grads)


def finish(first, last, win, gain_col, wn, dq, d_tm, dres, gi):
    gain = wide(gain_col)

    def step(i, carry):
        at = pl.ds(pl.multiple_of(i * CH, CH), CH)
        d = (
            nt(wn[:, pl.ds(L, 2 * L)], d_tm[at, pl.ds(0, 2 * L)])
            + nt(wn[:, pl.ds(4 * L, 2 * L)], d_tm[at, pl.ds(2 * L, 2 * L)])
            + nn(wn[:, pl.ds(0, L)], dq[pl.ds(0, L), at])
            + nn(wn[:, pl.ds(3 * L, L)], dq[pl.ds(L, L), at])
        )
        d = d.astype(BF16).astype(F32)[:C]
        xhat, inv = norm_parts(win[:, at].astype(F32)[:C])
        gi[:, at] = pad_rows(dres[:, at] + norm_back(xhat, inv, gain, d))
        return carry

    lax.fori_loop(first, last, step, 0, unroll=4)


def flips(value, count):
    out = [value]
    step = 1
    while step < count:
        bit = lax.rem(value // step, 2)
        out += [v + step - 2 * step * bit for v in out]
        step *= 2
    return out


class Spot:
    def __init__(self, clips, frames, xs, zs):
        self.zs = zs
        self.rows = 2 * zs * xs
        self.plane = clips * frames * xs
        self.clip, self.frame, self.row = (lax.axis_index(a) for a in ("clip", "frame", "row"))
        self.core = lax.rem(self.row, 2)
        self.z = lax.rem(self.row // 2, zs)
        self.q = (self.clip * frames + self.frame) * xs + self.row // (2 * zs)
        self.clips, self.frames = flips(self.clip, clips), flips(self.frame, frames)
        self.xs = [v * 2 * zs + self.z * 2 + self.core for v in flips(self.row // (2 * zs), xs)]
        self.qs = flips(self.q, self.plane)
        self.all = 2 * self.plane
        self.g = self.q * 2 + self.core
        self.gs = flips(self.g, self.all)

    def beside(self, frame_too, step):
        frame = self.frames[1] if frame_too else self.frame
        return self.clip, frame, lax.rem(self.row + step + self.rows, self.rows)

    def other_core(self):
        return self.clip, self.frame, self.row + 1 - 2 * self.core

    def in_plane(self, d):
        n, m = len(self.xs), len(self.frames)
        return self.clips[d // (n * m)], self.frames[d // n % m], self.xs[d % n]

    def in_both(self, d):
        clip, frame, row = self.in_plane(d // 2)
        return clip, frame, row + (d % 2) * (1 - 2 * self.core)

    def in_column(self, d):
        z = lax.rem(self.z + d, self.zs)
        return self.clip, self.frame, self.row + (z - self.z) * 2


def remote(src, dst, send, recv, to):
    return pltpu.make_async_remote_copy(
        src_ref=src, dst_ref=dst, send_sem=send, recv_sem=recv, device_id=to, device_id_type=MESH
    )


class Stream:
    def __init__(self, s, spot, r):
        self.s, self.at, self.r = s, spot, r
        self.block = HALF // spot.plane

    def sems(self, phase):
        return self.r["sem_send"].at[self.s, phase], self.r["sem_got"].at[self.s, phase]

    def half(self, core):
        return pl.ds(pl.multiple_of(self.s * 2 * HALF + core * HALF, HALF), HALF)

    def rows(self, q):
        return pl.ds(pl.multiple_of(q * self.block, self.block), self.block)

    def total_rows(self, q):
        first = self.s * 2 * HALF + self.at.core * HALF + q * self.block
        return pl.ds(pl.multiple_of(first, self.block), self.block)

    def pair(self):
        src = self.r["pack"].at[self.half(1 - self.at.core)]
        return remote(src, self.r["pair_got"].at[self.s], *self.sems(0), self.at.other_core())

    def scatter(self, d):
        r, s = self.r, self.s
        src = r["chip"].at[s, self.at.qs[d]]
        return remote(src, r["plane_got"].at[s, d - 1], *self.sems(1), self.at.in_plane(d))

    def scatters(self):
        r, s, rest = self.r, self.s, pl.ds(0, self.at.plane - 1)
        return remote(
            r["chip"].at[s, rest], r["plane_got"].at[s, rest], *self.sems(1), self.at.other_core()
        )

    def column(self, d):
        r, s = self.r, self.s
        dst = r["column_got"].at[s, self.at.z]
        return remote(r["mine"].at[s], dst, *self.sems(2), self.at.in_column(d))

    def columns(self):
        ref = self.r["column_got"].at[self.s, pl.ds(0, self.at.zs - 1)]
        return remote(ref, ref, *self.sems(2), self.at.other_core())

    def gather(self, d):
        ref = self.r["total"].at[self.total_rows(self.at.q)]
        return remote(ref, ref, *self.sems(3), self.at.in_plane(d))

    def gathers(self):
        rows = (self.at.plane - 1) * self.block
        ref = self.r["total"].at[pl.ds(self.s * 2 * HALF, rows)]
        return remote(ref, ref, *self.sems(3), self.at.other_core())

    def hand_over(self):
        ref = self.r["total"].at[self.half(self.at.core)]
        return remote(ref, ref, *self.sems(4), self.at.other_core())

    def step_pair(self):
        self.pair().start()

    def step_scatter(self):
        r, s = self.r, self.s
        self.pair().wait_recv()
        own = r["pack"][self.half(self.at.core), :].astype(F32)
        own = (own + r["pair_got"][s].astype(F32)).astype(BF16)
        r["chip"][s] = own.reshape(self.at.plane, self.block, L)
        for d in range(1, self.at.plane):
            self.scatter(d).start()

    def step_column(self):
        r, s = self.r, self.s
        self.scatters().wait_recv()
        total = r["chip"][s, self.at.q].astype(F32)
        for d in range(self.at.plane - 1):
            total = total + r["plane_got"][s, d].astype(F32)
        total = total.astype(BF16)
        r["mine"][s] = total
        r["column_got"][s, self.at.z] = total
        for d in range(1, self.at.zs):
            self.column(d).start()

    def step_gather(self):
        r, s = self.r, self.s
        self.columns().wait_recv()
        total = r["column_got"][s, 0].astype(F32)
        for i in range(1, self.at.zs):
            total = total + r["column_got"][s, i].astype(F32)
        r["total"][self.total_rows(self.at.q), :] = total.astype(BF16)
        for d in range(1, self.at.plane):
            self.gather(d).start()

    def step_hand_over(self):
        self.gathers().wait_recv()
        self.hand_over().start()

    def step_end(self):
        self.hand_over().wait_recv()
        self.pair().wait_send()
        self.scatters().wait_send()
        self.columns().wait_send()
        self.gathers().wait_send()
        self.hand_over().wait_send()


class Direct:
    def __init__(self, s, spot, r):
        self.s, self.at, self.r = s, spot, r
        self.block = HALF // spot.all

    def sems(self, phase):
        return self.r["direct_send"].at[self.s, phase], self.r["direct_got"].at[self.s, phase]

    def rows(self, g):
        first = 2 * HALF + self.s * HALF + g * self.block
        return pl.ds(pl.multiple_of(first, self.block), self.block)

    def scatter(self, d):
        r, s = self.r, self.s
        src = r["pack"].at[self.rows(self.at.gs[d])]
        return remote(src, r["all_got"].at[s, d - 1], *self.sems(0), self.at.in_both(d))

    def scatters(self):
        ref = self.r["all_got"].at[self.s]
        return remote(ref, ref, *self.sems(0), self.at.other_core())

    def column(self, d):
        r, s = self.r, self.s
        dst = r["height_got"].at[s, self.at.z]
        return remote(r["part_sum"].at[s], dst, *self.sems(1), self.at.in_column(d))

    def columns(self):
        ref = self.r["height_got"].at[self.s, pl.ds(0, self.at.zs - 1)]
        return remote(ref, ref, *self.sems(1), self.at.other_core())

    def gather(self, d):
        ref = self.r["total"].at[self.rows(self.at.g)]
        return remote(ref, ref, *self.sems(2), self.at.in_both(d))

    def gathers(self):
        rows = (self.at.all - 1) * self.block
        ref = self.r["total"].at[pl.ds(2 * HALF + self.s * HALF, rows)]
        return remote(ref, ref, *self.sems(2), self.at.other_core())

    def step_scatter(self):
        for d in range(1, self.at.all):
            self.scatter(d).start()

    def step_column(self):
        r, s = self.r, self.s
        self.scatters().wait_recv()
        total = r["pack"][self.rows(self.at.g), :].astype(F32)
        for d in range(self.at.all - 1):
            total = total + r["all_got"][s, d].astype(F32)
        total = total.astype(BF16)
        r["part_sum"][s] = total
        r["height_got"][s, self.at.z] = total
        for d in range(1, self.at.zs):
            self.column(d).start()

    def step_gather(self):
        r, s = self.r, self.s
        self.columns().wait_recv()
        total = r["height_got"][s, 0].astype(F32)
        for i in range(1, self.at.zs):
            total = total + r["height_got"][s, i].astype(F32)
        r["total"][self.rows(self.at.g), :] = total.astype(BF16)
        for d in range(1, self.at.all):
            self.gather(d).start()

    def step_end(self):
        self.gathers().wait_recv()
        self.scatters().wait_send()
        self.columns().wait_send()
        self.gathers().wait_send()


def layer_kernel(sizes, names, *refs):
    r = dict(zip(names, refs, strict=True))
    spot = Spot(*sizes)

    def get(*wanted):
        return [r[name] for name in wanted]

    barrier = pltpu.get_barrier_semaphore()

    def greet(to):
        pl.semaphore_signal(barrier, inc=1, device_id=to, device_id_type=MESH)

    for frame_too in (False, True):
        for step in (-1, 1):
            greet(spot.beside(frame_too, step))
    for d in range(1, spot.plane):
        greet(spot.in_plane(d))
    for d in range(1, spot.zs):
        greet(spot.in_column(d))

    bit = lax.rem(spot.frame, 2)
    sh, rh = r["sh"], r["rh"]
    split, join = get("split", "join")

    def outward(kind, pick):
        ends = [
            (3 - bit, 2 * bit + 1, spot.beside(True, -1)),
            (1 - bit, 2 * bit, spot.beside(True, 0)),
            (2 + bit, 2 * bit + 1, spot.beside(False, -1)),
        ]
        return [
            remote(*pick(src, dst), sh.at[kind, i], rh.at[kind, i], to)
            for i, (src, dst, to) in enumerate(ends)
        ]

    def homeward(kind, pick):
        ends = [
            (2 * (1 - bit) + 1, 2 + bit, spot.beside(True, 1)),
            (2 * (1 - bit), bit, spot.beside(True, 0)),
            (2 * bit + 1, 2 + bit, spot.beside(False, 1)),
        ]
        return [
            remote(*pick(src, dst), sh.at[kind, i], rh.at[kind, i], to)
            for i, (src, dst, to) in enumerate(ends)
        ]

    x_send, x_got, d_send, d_got = get("x_send", "x_got", "d_send", "d_got")
    g_send, g_got = get("g_send", "g_got")
    x_copies = [
        outward(u, lambda a, b, u=u: (x_send.at[u, a], x_got.at[u, b])) for u in range(2)
    ]
    d_copies = outward(2, lambda a, b: (d_send.at[:, a], d_got.at[:, b]))
    g_copies = homeward(3, lambda a, b: (g_send.at[:, a], g_got.at[:, b]))
    copies = x_copies[0] + x_copies[1] + d_copies + g_copies

    make_perms(split, join)
    for name, rows in (("x_slab", "x"), ("d_slab", "d_out")):
        for part in range(2):
            r[name][pl.ds(part * L + C, L - C), :] = jnp.zeros((L - C, HALF), BF16)
        to_slab(r[name], r[rows].at[0, 0])
    split_blocks(r["x_slab"], split, x_send)
    for u in range(2):
        x_got[u, 2 * bit] = x_send[u, bit]
    split_blocks(r["d_slab"], split, d_send)
    for u in range(2):
        d_got[u, 2 * bit] = d_send[u, bit]
    make_masks(*get("mask_h", "mask_f"))
    make_weights(
        *get("w_self", "w_mut", "w_proj", "f1", "f2", "w_down"),
        *get("wn", "wt", "proj", "proj_t", "fc_n", "fc_t", "down"),
    )
    make_gain(r["g1"], r["col1"])
    make_gain(r["g2"], r["col2"])
    pl.semaphore_wait(barrier, 4 + spot.plane - 1 + spot.zs - 1)
    for copy in x_copies[0] + x_copies[1]:
        copy.start()
    for u in range(2):
        for copy in x_copies[u]:
            copy.wait_recv()
        if u == 1:
            for copy in d_copies:
                copy.start()
        join_blocks(u, x_got, join, r["win"])
        norm_one(u, *get("win", "col1", "n_cm", "n_tm"))
        project(u, *get("wt", "wn", "n_cm", "n_tm", "cm", "tm"))
    attend(*get("cm", "tm", "mask_h", "mask_f", "probs", "joined"))
    for copy in d_copies:
        copy.wait_recv()
    for u in range(2):
        join_blocks(u, d_got, join, r["d_win"])
    feed_forward(
        *get("win", "d_win", "joined", "col2", "proj", "proj_t", "fc_n", "fc_t", "down"),
        *get("hid", "dup", "n2", "datt", "dres", "dj", "acc"),
    )
    early_grads(*get("hid", "dup", "n2", "joined", "datt", "d_win", "acc", "pack"))
    early, cross, last = Stream(0, spot, r), Direct(0, spot, r), Direct(1, spot, r)
    early.step_pair()

    def in_cross(p):
        @pl.when(p == 3)
        def _():
            early.step_scatter()

    def in_self(p):
        @pl.when(p == 5)
        def _():
            early.step_column()

    back = get("cm", "tm", "mask_h", "probs", "dj", "dq", "d_tm")
    back_cross(*back, r["mask_f"], in_cross)
    cross_grads(*get("n_cm", "dq", "d_tm", "wn", "pack", "acc"))
    cross.step_scatter()
    back_self(*back, in_self)
    self_grads(*get("n_cm", "dq", "d_tm", "wn", "pack", "acc", "col1"))
    last.step_scatter()
    finish(0, 4, *get("win", "col1", "wn", "dq", "d_tm", "dres", "gi"))
    gi, out = get("gi", "out")
    for u in range(2):
        blocks = nt(gi[:, pl.ds(u * HALF, HALF)], join[...]).astype(BF16)
        for s in range(4):
            g_send[u, s] = blocks[:, s * L : (s + 1) * L]
        g_got[u, bit] = g_send[u, 2 * bit]
    cross.step_column()
    early.step_gather()
    last.step_column()
    for copy in g_copies:
        copy.start()
    cross.step_gather()
    last.step_gather()
    for copy in g_copies:
        copy.wait_recv()
    for part in range(2):
        both = [g_got[u, 2 * part + half] for half in range(2) for u in range(2)]
        rows = nt(jnp.concatenate(both, axis=1), split[...]).astype(BF16)
        for i in range(4):
            out[4 * (1 - part) + i] = rows[:C, i * W : (i + 1) * W]
    early.step_hand_over()
    cross.step_end()
    early.step_end()
    last.step_end()
    for copy in copies:
        copy.wait_send()


def unpack_kernel(scale, total, gi, out, o1, o_self, o_mut, o_proj, o2, o_f1, o_f2, o_down):
    def block(i):
        return total[pl.ds(i * L, L), :].astype(F32) * scale

    def beside(parts):
        wide_parts = [
            jnp.concatenate([p, jnp.zeros((L, 2 * L), F32)], axis=1) for p in parts
        ]
        joined = wide_parts[0] + pltpu.roll(wide_parts[1], C, 1) + pltpu.roll(wide_parts[2], 2 * C, 1)
        return joined[:C, : 3 * C]

    b = [block(i) for i in range(8 + 3 + 4)]
    o_down[...] = jnp.concatenate([b[0], b[1]], axis=0)[:MLP, :C]
    o2[...] = b[1][MLP - L : MLP - L + 1, :C]
    o_f1[...] = jnp.concatenate([b[2], b[3]], axis=1)[:C, :MLP]
    o_f2[...] = jnp.concatenate([b[4], b[5]], axis=1)[:C, :MLP]
    o_proj[...] = jnp.concatenate([b[6][:C], b[7][:C]], axis=0)[:, :C]
    o1[...] = b[12][C : C + 1, :C]
    o_mut[...] = beside(b[8:11])
    o_self[...] = beside(b[12:15])
    out[0, 0] = gi[...]


def vmem(*shape, dtype=BF16):
    return pltpu.VMEM(shape, dtype)


def shape(*dims, dtype=BF16):
    return jax.ShapeDtypeStruct(dims, dtype)


def in_vmem(count):
    return [pl.BlockSpec(memory_space=pltpu.VMEM)] * count


def solution(mesh):
    clips, frames, rows = mesh.shape["clip"], mesh.shape["frame"], mesh.shape["row"]
    zs = min(8, rows // 2)
    xs = rows // (2 * zs)
    sizes = (clips, frames, xs, zs)
    plane = clips * frames * xs
    dma = pltpu.SemaphoreType.DMA
    ins = ["x", "d_out", "g1", "w_self", "w_mut", "w_proj", "g2", "f1", "f2", "w_down"]
    scratch = dict(
        split=vmem(HALF, HALF), join=vmem(HALF, HALF), x_slab=vmem(2 * L, HALF), d_slab=vmem(2 * L, HALF),
        x_send=vmem(2, 4, L, L), x_got=vmem(2, 4, L, L), d_send=vmem(2, 4, L, L), d_got=vmem(2, 4, L, L),
        g_send=vmem(2, 4, L, L), g_got=vmem(2, 4, L, L), win=vmem(L, T), d_win=vmem(L, T),
        mask_h=vmem(L, HEADS * L), mask_f=vmem(L, HEADS * L),
        wn=vmem(L, 6 * L), wt=vmem(6 * L, L), proj=vmem(2 * L, L), proj_t=vmem(L, 2 * L),
        fc_n=vmem(L, 2 * M), fc_t=vmem(2 * M, L), down=vmem(M, L),
        col1=vmem(C, L, dtype=F32), col2=vmem(C, L, dtype=F32), acc=vmem(C, L, dtype=F32),
        n_cm=vmem(L, T), n_tm=vmem(T, L), cm=vmem(6 * L, T), tm=vmem(T, 4 * L),
        probs=vmem(T // L, 2 * L, HEADS * L), joined=vmem(2 * L, T),
        hid=vmem(M, T), dup=vmem(2 * M, T), n2=vmem(L, T), datt=vmem(L, T),
        dres=vmem(C, T, dtype=F32), dj=vmem(2 * L, T),
        dq=vmem(2 * L, T), d_tm=vmem(T, 4 * L), gi=vmem(L, T),
        pack=vmem(ROWS, L), pair_got=vmem(1, HALF, L), chip=vmem(1, plane, HALF // plane, L),
        plane_got=vmem(1, plane - 1, HALF // plane, L), mine=vmem(1, HALF // plane, L),
        column_got=vmem(1, zs, HALF // plane, L),
        sh=dma((4, 3)), rh=dma((4, 3)), sem_send=dma((1, 5)), sem_got=dma((1, 5)),
        direct_send=dma((2, 3)), direct_got=dma((2, 3)), all_got=vmem(2, 2 * plane - 1, HALF // (2 * plane), L),
        part_sum=vmem(2, HALF // (2 * plane), L), height_got=vmem(2, zs, HALF // (2 * plane), L),
    )
    names = [*ins, "out", "total", *scratch]

    def on_device(x, d_out, g1, w_self, w_mut, w_proj, g2, f1, f2, w_down):
        g1, g2 = g1.reshape(1, C), g2.reshape(1, C)
        gi, total = pl.pallas_call(
            lambda *refs: layer_kernel(sizes, names, *refs),
            out_shape=(shape(8, C, W), shape(ROWS, L)),
            in_specs=in_vmem(10),
            out_specs=tuple(in_vmem(2)),
            scratch_shapes=list(scratch.values()),
            compiler_params=pltpu.CompilerParams(
                collective_id=0, has_side_effects=True, vmem_limit_bytes=56 * 2**20
            ),
        )(x, d_out, g1, w_self, w_mut, w_proj, g2, f1, f2, w_down)
        scale = float(T * rows * frames * clips) ** -0.5
        out = pl.pallas_call(
            lambda *refs: unpack_kernel(scale, *refs),
            out_shape=(
                shape(1, 1, 8, C, W), shape(1, C, dtype=F32), shape(C, 3 * C, dtype=F32),
                shape(C, 3 * C, dtype=F32), shape(2 * C, C, dtype=F32), shape(1, C, dtype=F32),
                shape(C, MLP, dtype=F32), shape(C, MLP, dtype=F32), shape(MLP, C, dtype=F32),
            ),
            in_specs=in_vmem(2),
            out_specs=tuple(in_vmem(9)),
            compiler_params=pltpu.CompilerParams(vmem_limit_bytes=56 * 2**20),
        )(total, gi)
        out = list(out)
        out[1], out[5] = out[1].reshape(C), out[5].reshape(C)
        return tuple(out)

    whole = P("clip", "frame", "row", None, None)
    return jax.shard_map(
        on_device,
        mesh=mesh,
        in_specs=(whole, whole) + (P(),) * 8,
        out_specs=(whole,) + (P(),) * 8,
        check_vma=False,
    )
```

profile of v0, /device:TPU:1, one launch (start us, length us, event | category | flops | bytes accessed | tf_op | source)
XLA Modules:
  0.0 51.9 jit_solution(10421765317763420558)
XLA Ops:
  0.6 49.1 %shard_map.169 = (bf16[8,120,128]{2,1,0:T(8,128)(2,1)}, bf16[2048,128]{1,0:T(8,128)(2,1)}) custom-call(bf16[1,1,8,120,128]{4,3,2,1,0:T(8,128)(2,1)} %refs_0_.1, bf16[1,1,8,120,128]{4,3,2,1,0:T(8,128)(2,1)} %refs_1_.1, f32[1,120]{1,0:T(1,128)} %bitcast.4, bf16[120,360]{1,0:T(8,128)(2,1)} %refs_3_.1, bf16[120,360]{1,0:T(8,128)(2,1)} %refs_4_.1, ...), custom_call_target="tpu_custom_call" | custom-call | tf_op jit(solution)/shard_map/pallas_call | solution.py:789
  49.7 2.2 %shard_map.170 = (bf16[1,1,8,120,128]{4,3,2,1,0:T(8,128)(2,1)}, f32[1,120]{1,0:T(1,128)}, f32[120,360]{1,0:T(8,128)}, f32[120,360]{1,0:T(8,128)}, f32[240,120]{1...) custom-call(bf16[2048,128]{1,0:T(8,128)(2,1)} %get-tuple-element.20.refs_0_, ...), custom_call_target="tpu_custom_call" | custom-call | tf_op jit(solution)/shard_map/pallas_call | solution.py:800
where the time goes:
time: 52 us; the launch traced here: 51.9 us
  Pallas kernels  51.2 us (98%)
  between operations  0.65 us (1%)
    pallas_call x1, Pallas kernels, on_device(): pl.pallas_call(lambda *refs: layer_kernel(sizes, names, *refs), out_shape...  49.1 us
    pallas_call x1, Pallas kernels, on_device(): pl.pallas_call(lambda *refs: unpack_kernel(scale, *refs), out_shape=(shap...  2.15 us

commit v1 on v0

--- a/solution.py
+++ b/solution.py
@@ -359,6 +359,13 @@
     return out
 
 
+RING = (0, 1, 2, 1)
+
+
+def farthest(count, hops):
+    return sorted(range(1, count), key=hops, reverse=True)
+
+
 class Spot:
     def __init__(self, clips, frames, xs, zs):
         self.zs = zs
@@ -375,6 +382,15 @@
         self.g = self.q * 2 + self.core
         self.gs = flips(self.g, self.all)
 
+        n, m = xs, frames
+
+        def hops(d):
+            return RING[(d // (n * m) * 2 + d % n) % 4] + RING[d // n % m % 4]
+
+        self.plane_order = farthest(self.plane, hops)
+        self.both_order = farthest(self.all, lambda d: hops(d // 2))
+        self.column_order = farthest(zs, lambda d: min(d, zs - d))
+
     def beside(self, frame_too, step):
         frame = self.frames[1] if frame_too else self.frame
         return self.clip, frame, lax.rem(self.row + step + self.rows, self.rows)
@@ -465,7 +481,7 @@
         own = r["pack"][self.half(self.at.core), :].astype(F32)
         own = (own + r["pair_got"][s].astype(F32)).astype(BF16)
         r["chip"][s] = own.reshape(self.at.plane, self.block, L)
-        for d in range(1, self.at.plane):
+        for d in self.at.plane_order:
             self.scatter(d).start()
 
     def step_column(self):
@@ -477,7 +493,7 @@
         total = total.astype(BF16)
         r["mine"][s] = total
         r["column_got"][s, self.at.z] = total
-        for d in range(1, self.at.zs):
+        for d in self.at.column_order:
             self.column(d).start()
 
     def step_gather(self):
@@ -487,7 +503,7 @@
         for i in range(1, self.at.zs):
             total = total + r["column_got"][s, i].astype(F32)
         r["total"][self.total_rows(self.at.q), :] = total.astype(BF16)
-        for d in range(1, self.at.plane):
+        for d in self.at.plane_order:
             self.gather(d).start()
 
     def step_hand_over(self):
@@ -543,7 +559,7 @@
         return remote(ref, ref, *self.sems(2), self.at.other_core())
 
     def step_scatter(self):
-        for d in range(1, self.at.all):
+        for d in self.at.both_order:
             self.scatter(d).start()
 
     def step_column(self):
@@ -555,7 +571,7 @@
         total = total.astype(BF16)
         r["part_sum"][s] = total
         r["height_got"][s, self.at.z] = total
-        for d in range(1, self.at.zs):
+        for d in self.at.column_order:
             self.column(d).start()
 
     def step_gather(self):
@@ -565,7 +581,7 @@
         for i in range(1, self.at.zs):
             total = total + r["height_got"][s, i].astype(F32)
         r["total"][self.rows(self.at.g), :] = total.astype(BF16)
-        for d in range(1, self.at.all):
+        for d in self.at.both_order:
             self.gather(d).start()
 
     def step_end(self):

time: 52 us -> 51.1 us (0.983)
  Pallas kernels: 51.2 us -> 50.3 us
    pallas_call x1, Pallas kernels: 49.1 us -> 48.1 us  [on_device(): pl.pallas_call(lambda *refs: layer_kernel(sizes, names, *refs), out_shape...]
where the time goes in v1:
time: 51.1 us; the launch traced here: 51 us
  Pallas kernels  50.3 us (98%)
  between operations  0.65 us (1%)
    pallas_call x1, Pallas kernels, on_device(): pl.pallas_call(lambda *refs: layer_kernel(sizes, names, *refs), out_shape...  48.1 us
    pallas_call x1, Pallas kernels, on_device(): pl.pallas_call(lambda *refs: unpack_kernel(scale, *refs), out_shape=(shap...  2.15 us

profile of v1, /device:TPU:1, one launch (start us, length us, event | category | flops | bytes accessed | tf_op | source)
XLA Modules:
  0.0 51.0 jit_solution(16998743691102032967)
XLA Ops:
  0.6 48.1 %shard_map.169 = (bf16[8,120,128]{2,1,0:T(8,128)(2,1)}, bf16[2048,128]{1,0:T(8,128)(2,1)}) custom-call(bf16[1,1,8,120,128]{4,3,2,1,0:T(8,128)(2,1)} %refs_0_.1, bf16[1,1,8,120,128]{4,3,2,1,0:T(8,128)(2,1)} %refs_1_.1, f32[1,120]{1,0:T(1,128)} %bitcast.4, bf16[120,360]{1,0:T(8,128)(2,1)} %refs_3_.1, bf16[120,360]{1,0:T(8,128)(2,1)} %refs_4_.1, ...), custom_call_target="tpu_custom_call" | custom-call | tf_op jit(solution)/shard_map/pallas_call | solution.py:805
  48.8 2.2 %shard_map.170 = (bf16[1,1,8,120,128]{4,3,2,1,0:T(8,128)(2,1)}, f32[1,120]{1,0:T(1,128)}, f32[120,360]{1,0:T(8,128)}, f32[120,360]{1,0:T(8,128)}, f32[240,120]{1...) custom-call(bf16[2048,128]{1,0:T(8,128)(2,1)} %get-tuple-element.20.refs_0_, ...), custom_call_target="tpu_custom_call" | custom-call | tf_op jit(solution)/shard_map/pallas_call | solution.py:816
